TPU v7x, 32 devices: a whole 2x2x4 slice. The times are simulated.
32 devices in a mesh: section: 1, expert: 32 (over z, y, x, core).
Axes of the slice: x: 2, y: 2, z: 4, core: 2. Of those that a mesh axis runs over, the one named last changes fastest.
Arguments:
- hidden: bfloat16 [1, 256, 7168], P('section', 'expert'), may hold values from -6 to 6
- norm_gain: float32 [1, 7168], P('section'), may hold values from 0.25 to 1.75
- w_up: bfloat16 [1, 7168, 4096], P('section', None, 'expert'), may hold values from -0.0625 to 0.0625
- w_down: bfloat16 [1, 4096, 7168], P('section', 'expert'), may hold values from -0.1875 to 0.1875
- expert_ids: int32 [1, 2, 256, 2], P('section', None, 'expert'), may hold values from 0 to 3, all different within a row; in each aligned block of 8 rows (0 to 7, 8 to 15, ..., all dimensions but the last counted through in order) at most 6 rows name the same one
- route_gates: float32 [1, 2, 256, 2], P('section', None, 'expert'), may hold values from 0.25 to 1.5
Outputs:
- advanced: bfloat16 [1, 256, 7168], P('section', 'expert')
Inputs may be any that keep to these rules, and one draw needn't show every extreme that they name: `expert_ids`: the 2 ids of a row differ. In each aligned block of 8 rows (the rows of one device in one pass) no expert is named by more than 6 rows; some expert is named by exactly 6 rows.
All inputs are finite; a program needn't handle non-finite values.
Results may differ from a plain program's by a relative error of at most 0.0085.
Values may be sent and summed in bfloat16 or wider, within the bound.
A program may use at most 64 MiB of HBM per device.

v0:
```python
import functools

import jax
import jax.numpy as jnp
from jax import lax
from jax.experimental import pallas as pl
from jax.experimental.pallas import tpu as pltpu
from jax.sharding import PartitionSpec as P

HID = 1024
HID_DEV = 128
CHUNKS = 4
WINDOW = 2
CHIPS = HID // HID_DEV // 2


def kernel(
    planes, sections, passes, cap,
    hidden, gain, ids, gates, up_hbm, down_hbm, out,
    up, down, column, rows, meta, slot_gates, part, first, second_out, second, plane_sum, plane_in, cur, shift_out, shift_in,
    w_local, w_send, w_recv, meta_send, meta_recv, zag_send, zag_recv, pag_send, pag_recv,
    one_send, one_recv, two_send, two_recv, zrs_send, zrs_recv, sh_send, sh_recv,
):
    me = lax.axis_index("expert")
    core = lax.rem(me, 2)
    chip = lax.rem(me // 2, CHIPS)
    plane = me // (2 * CHIPS)
    half = cur.shape[2]
    wide = half // CHUNKS
    mate = {1: chip + 1 - 2 * lax.rem(chip, 2), 2: lax.rem(chip + 2, 4), 3: 3 - chip}

    def at(plane_index, chip_index, core_index):
        return {"expert": (plane_index * CHIPS + chip_index) * 2 + core_index}

    def plane_at(by):
        return lax.rem(plane + by + planes, planes)

    partner = at(plane, chip, 1 - core)
    peers = [at(plane_at(d), chip, core) for d in range(1, planes)]
    mates = {k: at(plane, mate[k], core) for k in (1, 2)}
    targets = [partner, mates[1], mates[2]] + peers
    if sections > 1:
        sec = lax.axis_index("section")
        after = {"section": lax.rem(sec + 1, sections)}
        before = {"section": lax.rem(sec + sections - 1, sections)}
        targets = targets + [after, before]
    barrier = pltpu.get_barrier_semaphore()
    for target in targets:
        pl.semaphore_signal(barrier, inc=1, device_id=target, device_id_type=pl.DeviceIdType.MESH)
    pl.semaphore_wait(barrier, len(targets))

    pending = []

    def remote(src, dst, send, recv, target):
        return pltpu.make_async_remote_copy(
            src_ref=src, dst_ref=dst, send_sem=send, recv_sem=recv,
            device_id=target, device_id_type=pl.DeviceIdType.MESH,
        )

    def send(*args):
        copy = remote(*args)
        copy.start()
        pending.append(copy)

    lanes = lax.broadcasted_iota(jnp.int32, (8, 128), 1)
    diagonal = lax.broadcasted_iota(jnp.int32, (8, 8), 0) == lax.broadcasted_iota(jnp.int32, (8, 8), 1)
    table = jnp.zeros((8, 128), jnp.float32)
    for p in range(passes):
        for k in range(ids.shape[1]):
            named = jnp.sum(jnp.where(diagonal, ids[p, k : k + 1, :], 0).astype(jnp.float32), axis=-1, keepdims=True)
            weight = jnp.sum(jnp.where(diagonal, gates[p, k : k + 1, :], 0.0), axis=-1, keepdims=True)
            hit = lanes == named.astype(jnp.int32) + p * planes
            table = table + jnp.where(hit, weight, 0.0)
    meta[plane] = table
    for d in range(1, planes):
        send(meta.at[plane], meta.at[plane], meta_send.at[d - 1], meta_recv.at[d - 1], peers[d - 1])

    for h in range(2):
        cur[h] = hidden[:, h * half : (h + 1) * half].astype(jnp.float32)

    def gather_z(p):
        a, b = cur[0], cur[1]
        total = jnp.sum(a * a, axis=-1, keepdims=True) + jnp.sum(b * b, axis=-1, keepdims=True)
        scale = lax.rsqrt(total / (2 * half) + 1e-06)
        for c in range(CHUNKS):
            lo, hi = c * wide, (c + 1) * wide
            top = cur[0, :, lo:hi] * scale * gain[:, lo:hi]
            bottom = cur[1, :, lo:hi] * scale * gain[:, half + lo : half + hi]
            column[p, c, plane] = jnp.concatenate([top, bottom], axis=0).astype(jnp.bfloat16)
        for c in range(WINDOW):
            start_z(p, c)

    def start_z(p, c):
        block = column.at[p, c, plane]
        for d in range(1, planes):
            send(block, block, zag_send.at[p, c, d - 1], zag_recv.at[p, c, d - 1], peers[d - 1])

    def order(c):
        return (1, 2) if c % 2 == 0 else (2, 1)

    gather_z(0)
    locals_ = [
        pltpu.make_async_copy(up_hbm, up.at[:, pl.ds(0, HID_DEV)], w_local.at[0]),
        pltpu.make_async_copy(down_hbm, down.at[pl.ds(0, HID_DEV)], w_local.at[1]),
    ]
    for copy in locals_:
        copy.start()
    up_copy = remote(up_hbm, up.at[:, pl.ds(HID_DEV, HID_DEV)], w_send.at[0], w_recv.at[0], partner)
    down_copy = remote(down_hbm, down.at[pl.ds(HID_DEV, HID_DEV)], w_send.at[1], w_recv.at[1], partner)
    up_copy.start()
    down_copy.start()

    for d in range(1, planes):
        src = meta.at[plane_at(-d)]
        remote(src, src, meta_send.at[d - 1], meta_recv.at[d - 1], peers[d - 1]).wait_recv()
    slots = planes * cap
    count = planes * 16
    unpackers, packers = [], []
    gate_lanes = jnp.zeros((slots, 128), jnp.float32)
    for p in range(passes):
        pieces = []
        for g in range(planes):
            gate = jnp.sum(jnp.where(lanes == plane + p * planes, meta[g], 0.0), axis=-1, keepdims=True)
            routed = jnp.where(gate != 0.0, 1.0, 0.0)
            earlier = jnp.sum(
                jnp.where(
                    lax.broadcasted_iota(jnp.int32, (8, 8), 0) < lax.broadcasted_iota(jnp.int32, (8, 8), 1), routed, 0.0
                ),
                axis=0, keepdims=True,
            )
            place = jnp.sum(jnp.where(diagonal, earlier, 0.0), axis=-1, keepdims=True).astype(jnp.int32)
            for h in range(2):
                pieces.append(jnp.where(lanes == place + (h * slots + g * cap), gate, 0.0))
        if count < 128:
            pieces.append(jnp.zeros((128 - count, 128), jnp.float32))
        spread = jnp.concatenate(pieces, axis=0)
        turned = spread.T
        unpackers.append(jnp.where(spread[:count, : 2 * slots] != 0.0, 1.0, 0.0).astype(jnp.bfloat16))
        packers.append(jnp.where(turned[: 2 * slots, :count] != 0.0, 1.0, 0.0).astype(jnp.bfloat16))
        slot_gate = jnp.sum(turned[:slots], axis=-1, keepdims=True)
        gate_lanes = gate_lanes + jnp.where(lax.broadcasted_iota(jnp.int32, (slots, 128), 1) == p, slot_gate, 0.0)
    slot_gates[chip] = gate_lanes
    slot = planes - 1
    for i, k in enumerate((1, 2)):
        send(slot_gates.at[chip], slot_gates.at[chip], meta_send.at[slot + i], meta_recv.at[slot + i], mates[k])

    def meta_forward():
        src = slot_gates.at[mate[1]]
        remote(src, src, meta_send.at[slot], meta_recv.at[slot], mates[1]).wait_recv()
        send(src, src, meta_send.at[slot + 2], meta_recv.at[slot + 2], mates[2])

    def meta_finish():
        for i, k in ((1, 2), (2, 3)):
            src = slot_gates.at[mate[k]]
            remote(src, src, meta_send.at[slot + i], meta_recv.at[slot + i], mates[2]).wait_recv()

    for p in range(passes):
        if p > 0:
            gather_z(p)
        top_sum = bottom_sum = None
        for step in range(CHUNKS + 2):
            if step < CHUNKS:
                c = step
                for d in range(1, planes):
                    src = column.at[p, c, plane_at(-d)]
                    remote(src, src, zag_send.at[p, c, d - 1], zag_recv.at[p, c, d - 1], peers[d - 1]).wait_recv()
                if c + WINDOW < CHUNKS:
                    start_z(p, c + WINDOW)
                rows[p, c, chip] = jnp.dot(
                    packers[p], column[p, c].reshape(count, wide), preferred_element_type=jnp.float32
                ).astype(jnp.bfloat16)
                for i, k in enumerate(order(c)):
                    src = rows.at[p, c, chip]
                    send(src, src, pag_send.at[p, c, i], pag_recv.at[p, c, i], mates[k])
            if 1 <= step <= CHUNKS:
                c = step - 1
                near, far = order(c)
                src = rows.at[p, c, mate[near]]
                remote(src, src, pag_send.at[p, c, 0], pag_recv.at[p, c, 0], mates[near]).wait_recv()
                send(src, src, pag_send.at[p, c, 2], pag_recv.at[p, c, 2], mates[far])
                if p == 0 and step == 1:
                    meta_forward()
            if step >= 2:
                c = step - 2
                near, far = order(c)
                for i, k in ((1, far), (2, 3)):
                    src = rows.at[p, c, mate[k]]
                    remote(src, src, pag_send.at[p, c, i], pag_recv.at[p, c, i], mates[far]).wait_recv()
                if p == 0 and c == 0:
                    locals_[0].wait()
                    up_copy.wait_recv()
                block = rows[p, c].reshape(CHIPS * 2 * slots, wide)
                top = jnp.dot(block, up[c * wide : (c + 1) * wide, :], preferred_element_type=jnp.float32)
                bottom = jnp.dot(
                    block, up[half + c * wide : half + (c + 1) * wide, :], preferred_element_type=jnp.float32
                )
                top_sum = top if c == 0 else top_sum + top
                bottom_sum = bottom if c == 0 else bottom_sum + bottom
        if p == 0:
            meta_finish()
            locals_[1].wait()
            down_copy.wait_recv()
        upward = (
            top_sum.reshape(CHIPS, 2, slots, 2 * HID_DEV)[:, 0]
            + bottom_sum.reshape(CHIPS, 2, slots, 2 * HID_DEV)[:, 1]
        ).reshape(CHIPS * slots, 2 * HID_DEV)
        gate = slot_gates[...].reshape(CHIPS * slots, 128)[:, p : p + 1]
        active = (upward / (1.0 + jnp.exp(-upward)) * gate).astype(jnp.bfloat16)

        def start_down(c):
            lo, hi = c * wide, (c + 1) * wide
            top = jnp.dot(active, down[:, lo:hi], preferred_element_type=jnp.float32)
            bottom = jnp.dot(active, down[:, half + lo : half + hi], preferred_element_type=jnp.float32)
            both = jnp.concatenate(
                [top.reshape(CHIPS, slots, wide), bottom.reshape(CHIPS, slots, wide)], axis=1
            )
            part[p, c] = both.astype(jnp.bfloat16)
            near, far = order(c)
            for i, k in ((1, 3), (0, near)):
                send(
                    part.at[p, c, mate[k]], first.at[p, c, i], one_send.at[p, c, i], one_recv.at[p, c, i], mates[near]
                )

        for c in range(WINDOW):
            start_down(c)
        for step in range(CHUNKS + 1):
            if step < CHUNKS:
                c = step
                near, far = order(c)
                src = first.at[p, c, 1]
                remote(src, src, one_send.at[p, c, 1], one_recv.at[p, c, 1], mates[near]).wait_recv()
                total = part[p, c, mate[far]].astype(jnp.float32) + first[p, c, 1].astype(jnp.float32)
                second_out[p, c] = total.astype(jnp.bfloat16)
                send(second_out.at[p, c], second.at[p, c], two_send.at[p, c], two_recv.at[p, c], mates[far])
                if c + WINDOW < CHUNKS:
                    start_down(c + WINDOW)
            if step >= 1:
                c = step - 1
                near, far = order(c)
                src = first.at[p, c, 0]
                remote(src, src, one_send.at[p, c, 0], one_recv.at[p, c, 0], mates[near]).wait_recv()
                src = second.at[p, c]
                remote(src, src, two_send.at[p, c], two_recv.at[p, c], mates[far]).wait_recv()
                total = part[p, c, chip].astype(jnp.float32) + first[p, c, 0].astype(jnp.float32)
                total = total + second[p, c].astype(jnp.float32)
                unpacked = jnp.dot(unpackers[p], total.astype(jnp.bfloat16), preferred_element_type=jnp.float32)
                plane_sum[p, c] = unpacked.astype(jnp.bfloat16).reshape(planes, 16, wide)
                for d in range(1, planes):
                    send(
                        plane_sum.at[p, c, plane_at(d)], plane_in.at[p, c, d - 1],
                        zrs_send.at[p, c, d - 1], zrs_recv.at[p, c, d - 1], peers[d - 1],
                    )
        for c in range(CHUNKS):
            lo, hi = c * wide, (c + 1) * wide
            total = plane_sum[p, c, plane].astype(jnp.float32)
            for d in range(1, planes):
                src = plane_in.at[p, c, d - 1]
                remote(src, src, zrs_send.at[p, c, d - 1], zrs_recv.at[p, c, d - 1], peers[d - 1]).wait_recv()
                total = total + plane_in[p, c, d - 1].astype(jnp.float32)
            for h in range(2):
                value = (cur[h, :, lo:hi] + total[h * 8 : h * 8 + 8]).astype(jnp.bfloat16).astype(jnp.float32)
                cur[h, :, lo:hi] = value
        if sections > 1:
            shift_out[p] = jnp.concatenate([cur[0], cur[1]], axis=0).astype(jnp.bfloat16)
            send(shift_out.at[p], shift_in.at[p], sh_send.at[p], sh_recv.at[p], after)
            remote(shift_out.at[p], shift_in.at[p], sh_send.at[p], sh_recv.at[p], after).wait_recv()
            for h in range(2):
                cur[h] = shift_in[p].astype(jnp.float32)[h * 8 : h * 8 + 8]
    for h in range(2):
        out[:, h * half : (h + 1) * half] = cur[h].astype(jnp.bfloat16)
    up_copy.wait_send()
    down_copy.wait_send()
    for copy in pending:
        copy.wait_send()


def body(hidden, norm_gain, w_up, w_down, expert_ids, route_gates):
    width = hidden.shape[-1]
    half = width // 2
    wide = half // CHUNKS
    planes = lax.axis_size("expert") // (2 * CHIPS)
    sections = lax.axis_size("section")
    passes = expert_ids.shape[1]
    bf = jnp.bfloat16
    dma = pltpu.SemaphoreType.DMA
    away = planes - 1
    shift = passes if sections > 1 else 1
    routes = hidden.shape[1] * expert_ids.shape[-1]
    cap = min(hidden.shape[1], (routes + planes - 1) // planes + 2)
    slots = planes * cap
    vmem = pl.BlockSpec(memory_space=pltpu.VMEM)
    hbm = pl.BlockSpec(memory_space=pl.ANY)
    result = pl.pallas_call(
        functools.partial(kernel, planes, sections, passes, cap),
        out_shape=jax.ShapeDtypeStruct((8, width), bf),
        in_specs=[vmem] * 4 + [hbm] * 2,
        out_specs=vmem,
        scratch_shapes=[
            pltpu.VMEM((width, 2 * HID_DEV), bf),
            pltpu.VMEM((2 * HID_DEV, width), bf),
            pltpu.VMEM((passes, CHUNKS, planes, 16, wide), bf),
            pltpu.VMEM((passes, CHUNKS, CHIPS, 2 * slots, wide), bf),
            pltpu.VMEM((planes, 8, 128), jnp.float32),
            pltpu.VMEM((CHIPS, slots, 128), jnp.float32),
            pltpu.VMEM((passes, CHUNKS, CHIPS, 2 * slots, wide), bf),
            pltpu.VMEM((passes, CHUNKS, 2, 2 * slots, wide), bf),
            pltpu.VMEM((passes, CHUNKS, 2 * slots, wide), bf),
            pltpu.VMEM((passes, CHUNKS, 2 * slots, wide), bf),
            pltpu.VMEM((passes, CHUNKS, planes, 16, wide), bf),
            pltpu.VMEM((passes, CHUNKS, away, 16, wide), bf),
            pltpu.VMEM((2, 8, half), jnp.float32),
            pltpu.VMEM((shift, 16, half), bf),
            pltpu.VMEM((shift, 16, half), bf),
            dma((2,)), dma((2,)), dma((2,)),
            dma((away + 3,)), dma((away + 3,)),
            dma((passes, CHUNKS, away)), dma((passes, CHUNKS, away)),
            dma((passes, CHUNKS, 3)), dma((passes, CHUNKS, 3)),
            dma((passes, CHUNKS, 2)), dma((passes, CHUNKS, 2)),
            dma((passes, CHUNKS)), dma((passes, CHUNKS)),
            dma((passes, CHUNKS, away)), dma((passes, CHUNKS, away)),
            dma((shift,)), dma((shift,)),
        ],
        compiler_params=pltpu.CompilerParams(
            collective_id=0, has_side_effects=True, vmem_limit_bytes=56 * 1024 * 1024
        ),
    )(
        hidden[0], norm_gain, expert_ids[0].swapaxes(1, 2), route_gates[0].swapaxes(1, 2), w_up[0], w_down[0]
    )
    return result[None]


def solution(mesh):
    placed = (
        P("section", "expert", None),
        P("section", None),
        P("section", None, "expert"),
        P("section", "expert", None),
        P("section", None, "expert", None),
        P("section", None, "expert", None),
    )
    return jax.shard_map(
        body, mesh=mesh, in_specs=placed, out_specs=P("section", "expert", None), check_vma=False
    )
```

profile of v0, /device:TPU:0, one launch (start us, length us, event | category | flops | bytes accessed | tf_op | source)
XLA Modules:
  0.0 92.2 jit_solution(3509601190962002986)
XLA Ops:
  0.0 90.6 %shard_map.64 = bf16[8,7168]{1,0:T(8,128)(2,1)} custom-call(bf16[8,7168]{1,0:T(8,128)(2,1)} %bitcast.13, f32[1,7168]{1,0:T(1,128)} %gain.1, s32[2,2,8]{2,1,0:T(2,128)} %bitcast.14, f32[2,2,8]{2,1,0:T(2,128)} %bitcast.15, bf16[7168,128]{1,0:T(8,128)(2,1)} %bitcast.10, bf16[128,7168]{1,0:T(8,128)(2,1)} %bitcast.11), custom_call_target="tpu_custom_call" | custom-call | tf_op jit(solution)/shard_map/pallas_call | solution.py:293
  90.6 1.6 %copy.8 = bf16[1,8,7168]{2,1,0:T(8,128)(2,1)} copy(bf16[1,8,7168]{2,1,0:T(8,128)(2,1)} %bitcast.12) | data formatting | bytes 229376
where the time goes:
time: 92.3 us; the launch traced here: 92.2 us
  Pallas kernels  90.6 us (98%)
  local copies, waits for them, and re-layouts  1.55 us (2%)
    pallas_call x1, Pallas kernels, body(): pl.pallas_call(functools.partial(kernel, planes, sections, passes, cap),...  90.6 us

commit v1 on v0

--- a/solution.py
+++ b/solution.py
@@ -17,9 +17,9 @@
 def kernel(
     planes, sections, passes, cap,
     hidden, gain, ids, gates, up_hbm, down_hbm, out,
-    up, down, column, rows, meta, slot_gates, part, first, second_out, second, plane_sum, plane_in, cur, shift_out, shift_in,
+    up, down, column, rows, meta, slot_gates, part, first, plane_sum, plane_in, cur, shift_out, shift_in,
     w_local, w_send, w_recv, meta_send, meta_recv, zag_send, zag_recv, pag_send, pag_recv,
-    one_send, one_recv, two_send, two_recv, zrs_send, zrs_recv, sh_send, sh_recv,
+    one_send, one_recv, zrs_send, zrs_recv, sh_send, sh_recv,
 ):
     me = lax.axis_index("expert")
     core = lax.rem(me, 2)
@@ -37,8 +37,8 @@
 
     partner = at(plane, chip, 1 - core)
     peers = [at(plane_at(d), chip, core) for d in range(1, planes)]
-    mates = {k: at(plane, mate[k], core) for k in (1, 2)}
-    targets = [partner, mates[1], mates[2]] + peers
+    mates = {k: at(plane, mate[k], core) for k in (1, 2, 3)}
+    targets = [partner, mates[1], mates[2], mates[3]] + peers
     if sections > 1:
         sec = lax.axis_index("section")
         after = {"section": lax.rem(sec + 1, sections)}
@@ -94,9 +94,6 @@
         block = column.at[p, c, plane]
         for d in range(1, planes):
             send(block, block, zag_send.at[p, c, d - 1], zag_recv.at[p, c, d - 1], peers[d - 1])
-
-    def order(c):
-        return (1, 2) if c % 2 == 0 else (2, 1)
 
     gather_z(0)
     locals_ = [
@@ -141,24 +138,20 @@
         gate_lanes = gate_lanes + jnp.where(lax.broadcasted_iota(jnp.int32, (slots, 128), 1) == p, slot_gate, 0.0)
     slot_gates[chip] = gate_lanes
     slot = planes - 1
-    for i, k in enumerate((1, 2)):
-        send(slot_gates.at[chip], slot_gates.at[chip], meta_send.at[slot + i], meta_recv.at[slot + i], mates[k])
-
-    def meta_forward():
-        src = slot_gates.at[mate[1]]
-        remote(src, src, meta_send.at[slot], meta_recv.at[slot], mates[1]).wait_recv()
-        send(src, src, meta_send.at[slot + 2], meta_recv.at[slot + 2], mates[2])
+    for k in (3, 1, 2):
+        src = slot_gates.at[chip]
+        send(src, src, meta_send.at[slot + k - 1], meta_recv.at[slot + k - 1], mates[k])
 
     def meta_finish():
-        for i, k in ((1, 2), (2, 3)):
+        for k in (1, 2, 3):
             src = slot_gates.at[mate[k]]
-            remote(src, src, meta_send.at[slot + i], meta_recv.at[slot + i], mates[2]).wait_recv()
+            remote(src, src, meta_send.at[slot + k - 1], meta_recv.at[slot + k - 1], mates[k]).wait_recv()
 
     for p in range(passes):
         if p > 0:
             gather_z(p)
         top_sum = bottom_sum = None
-        for step in range(CHUNKS + 2):
+        for step in range(CHUNKS + 1):
             if step < CHUNKS:
                 c = step
                 for d in range(1, planes):
@@ -169,23 +162,14 @@
                 rows[p, c, chip] = jnp.dot(
                     packers[p], column[p, c].reshape(count, wide), preferred_element_type=jnp.float32
                 ).astype(jnp.bfloat16)
-                for i, k in enumerate(order(c)):
+                for k in (3, 1, 2):
                     src = rows.at[p, c, chip]
-                    send(src, src, pag_send.at[p, c, i], pag_recv.at[p, c, i], mates[k])
-            if 1 <= step <= CHUNKS:
+                    send(src, src, pag_send.at[p, c, k - 1], pag_recv.at[p, c, k - 1], mates[k])
+            if step >= 1:
                 c = step - 1
-                near, far = order(c)
-                src = rows.at[p, c, mate[near]]
-                remote(src, src, pag_send.at[p, c, 0], pag_recv.at[p, c, 0], mates[near]).wait_recv()
-                send(src, src, pag_send.at[p, c, 2], pag_recv.at[p, c, 2], mates[far])
-                if p == 0 and step == 1:
-                    meta_forward()
-            if step >= 2:
-                c = step - 2
-                near, far = order(c)
-                for i, k in ((1, far), (2, 3)):
+                for k in (1, 2, 3):
                     src = rows.at[p, c, mate[k]]
-                    remote(src, src, pag_send.at[p, c, i], pag_recv.at[p, c, i], mates[far]).wait_recv()
+                    remote(src, src, pag_send.at[p, c, k - 1], pag_recv.at[p, c, k - 1], mates[k]).wait_recv()
                 if p == 0 and c == 0:
                     locals_[0].wait()
                     up_copy.wait_recv()
@@ -215,41 +199,29 @@
                 [top.reshape(CHIPS, slots, wide), bottom.reshape(CHIPS, slots, wide)], axis=1
             )
             part[p, c] = both.astype(jnp.bfloat16)
-            near, far = order(c)
-            for i, k in ((1, 3), (0, near)):
+            for k in (3, 1, 2):
                 send(
-                    part.at[p, c, mate[k]], first.at[p, c, i], one_send.at[p, c, i], one_recv.at[p, c, i], mates[near]
+                    part.at[p, c, mate[k]], first.at[p, c, k - 1],
+                    one_send.at[p, c, k - 1], one_recv.at[p, c, k - 1], mates[k],
                 )
 
         for c in range(WINDOW):
             start_down(c)
-        for step in range(CHUNKS + 1):
-            if step < CHUNKS:
-                c = step
-                near, far = order(c)
-                src = first.at[p, c, 1]
-                remote(src, src, one_send.at[p, c, 1], one_recv.at[p, c, 1], mates[near]).wait_recv()
-                total = part[p, c, mate[far]].astype(jnp.float32) + first[p, c, 1].astype(jnp.float32)
-                second_out[p, c] = total.astype(jnp.bfloat16)
-                send(second_out.at[p, c], second.at[p, c], two_send.at[p, c], two_recv.at[p, c], mates[far])
-                if c + WINDOW < CHUNKS:
-                    start_down(c + WINDOW)
-            if step >= 1:
-                c = step - 1
-                near, far = order(c)
-                src = first.at[p, c, 0]
-                remote(src, src, one_send.at[p, c, 0], one_recv.at[p, c, 0], mates[near]).wait_recv()
-                src = second.at[p, c]
-                remote(src, src, two_send.at[p, c], two_recv.at[p, c], mates[far]).wait_recv()
-                total = part[p, c, chip].astype(jnp.float32) + first[p, c, 0].astype(jnp.float32)
-                total = total + second[p, c].astype(jnp.float32)
-                unpacked = jnp.dot(unpackers[p], total.astype(jnp.bfloat16), preferred_element_type=jnp.float32)
-                plane_sum[p, c] = unpacked.astype(jnp.bfloat16).reshape(planes, 16, wide)
-                for d in range(1, planes):
-                    send(
-                        plane_sum.at[p, c, plane_at(d)], plane_in.at[p, c, d - 1],
-                        zrs_send.at[p, c, d - 1], zrs_recv.at[p, c, d - 1], peers[d - 1],
-                    )
+        for c in range(CHUNKS):
+            total = part[p, c, chip].astype(jnp.float32)
+            for k in (1, 2, 3):
+                src = first.at[p, c, k - 1]
+                remote(src, src, one_send.at[p, c, k - 1], one_recv.at[p, c, k - 1], mates[k]).wait_recv()
+                total = total + first[p, c, k - 1].astype(jnp.float32)
+            if c + WINDOW < CHUNKS:
+                start_down(c + WINDOW)
+            unpacked = jnp.dot(unpackers[p], total.astype(jnp.bfloat16), preferred_element_type=jnp.float32)
+            plane_sum[p, c] = unpacked.astype(jnp.bfloat16).reshape(planes, 16, wide)
+            for d in range(1, planes):
+                send(
+                    plane_sum.at[p, c, plane_at(d)], plane_in.at[p, c, d - 1],
+                    zrs_send.at[p, c, d - 1], zrs_recv.at[p, c, d - 1], peers[d - 1],
+                )
         for c in range(CHUNKS):
             lo, hi = c * wide, (c + 1) * wide
             total = plane_sum[p, c, plane].astype(jnp.float32)
@@ -303,9 +275,7 @@
             pltpu.VMEM((planes, 8, 128), jnp.float32),
             pltpu.VMEM((CHIPS, slots, 128), jnp.float32),
             pltpu.VMEM((passes, CHUNKS, CHIPS, 2 * slots, wide), bf),
-            pltpu.VMEM((passes, CHUNKS, 2, 2 * slots, wide), bf),
-            pltpu.VMEM((passes, CHUNKS, 2 * slots, wide), bf),
-            pltpu.VMEM((passes, CHUNKS, 2 * slots, wide), bf),
+            pltpu.VMEM((passes, CHUNKS, 3, 2 * slots, wide), bf),
             pltpu.VMEM((passes, CHUNKS, planes, 16, wide), bf),
             pltpu.VMEM((passes, CHUNKS, away, 16, wide), bf),
             pltpu.VMEM((2, 8, half), jnp.float32),
@@ -315,8 +285,7 @@
             dma((away + 3,)), dma((away + 3,)),
             dma((passes, CHUNKS, away)), dma((passes, CHUNKS, away)),
             dma((passes, CHUNKS, 3)), dma((passes, CHUNKS, 3)),
-            dma((passes, CHUNKS, 2)), dma((passes, CHUNKS, 2)),
-            dma((passes, CHUNKS)), dma((passes, CHUNKS)),
+            dma((passes, CHUNKS, 3)), dma((passes, CHUNKS, 3)),
             dma((passes, CHUNKS, away)), dma((passes, CHUNKS, away)),
             dma((shift,)), dma((shift,)),
         ],

time: 92.3 us -> 91.2 us (0.988)
  Pallas kernels: 90.6 us -> 89.5 us
    pallas_call x1, Pallas kernels: 90.6 us -> 89.5 us  [body(): pl.pallas_call(functools.partial(kernel, planes, sections, passes, cap),...]
where the time goes in v1:
time: 91.2 us; the launch traced here: 91.1 us
  Pallas kernels  89.5 us (98%)
  local copies, waits for them, and re-layouts  1.55 us (2%)
    pallas_call x1, Pallas kernels, body(): pl.pallas_call(functools.partial(kernel, planes, sections, passes, cap),...  89.5 us

profile of v1, /device:TPU:0, one launch (start us, length us, event | category | flops | bytes accessed | tf_op | source)
XLA Modules:
  0.0 91.1 jit_solution(10093400543041017058)
XLA Ops:
  0.0 89.5 %shard_map.64 = bf16[8,7168]{1,0:T(8,128)(2,1)} custom-call(bf16[8,7168]{1,0:T(8,128)(2,1)} %bitcast.13, f32[1,7168]{1,0:T(1,128)} %gain.1, s32[2,2,8]{2,1,0:T(2,128)} %bitcast.14, f32[2,2,8]{2,1,0:T(2,128)} %bitcast.15, bf16[7168,128]{1,0:T(8,128)(2,1)} %bitcast.10, bf16[128,7168]{1,0:T(8,128)(2,1)} %bitcast.11), custom_call_target="tpu_custom_call" | custom-call | tf_op jit(solution)/shard_map/pallas_call | solution.py:265
  89.5 1.6 %copy.8 = bf16[1,8,7168]{2,1,0:T(8,128)(2,1)} copy(bf16[1,8,7168]{2,1,0:T(8,128)(2,1)} %bitcast.12) | data formatting | bytes 229376
